TPU v7x, 32 devices: a whole 2x2x4 slice. The times are simulated.
32 devices in a mesh: tm: 8 (over z, y), row: 4 (over x, core).
Axes of the slice: x: 2, y: 2, z: 4, core: 2. Of those that a mesh axis runs over, the one named last changes fastest.
Arguments:
- edge_factor: float32 [8, 512, 512], P('tm', 'row'), may hold values from -0.25 to 0.25
- mass: float32 [8, 512], P('tm', 'row'), may hold values from 0.001 to 0.01
- rhs: float32 [8, 512, 512], P('tm', None, 'row'), may hold values from -0.25 to 0.25
Outputs:
- solution: float32 [8, 512, 512], P('tm', None, 'row')
All inputs are finite; a program needn't handle non-finite values.
Results may differ from a plain program's by a relative error of at most 0.0003.
Values sent between devices are 32-bit elements; how exact they have to be, the bound alone decides.
No kernel may reach another device: no remote copies, remote signals or barrier semaphores. Data moves between devices by JAX's collectives and lax.ppermute only.
A program may use at most 128 MiB of HBM per device.

v0:
```python
import jax
import jax.numpy as jnp
from jax import lax
from jax.sharding import PartitionSpec as P

exact_prec = lax.Precision.HIGHEST


def passed_along(block, axis, distance):
    devices = range(lax.axis_size(axis))
    route = [(i - distance, i) for i in devices if i - distance in devices]
    return lax.ppermute(block, axis, route)


def solve_lower(factor, values):
    return jax.scipy.linalg.solve_triangular(factor, values, lower=True)


def block_cholesky(matrix):
    half = matrix.shape[0] // 2
    upper_left = jnp.linalg.cholesky(matrix[:half, :half])
    lower_left = solve_lower(upper_left, matrix[:half, half:]).T
    schur_part = matrix[half:, half:] - jnp.dot(lower_left, lower_left.T, precision=exact_prec)
    lower_right = jnp.linalg.cholesky(schur_part)
    top_rows = jnp.concatenate(
        [upper_left, jnp.zeros((half, matrix.shape[0] - half), jnp.float32)], axis=1
    )
    bottom_rows = jnp.concatenate([lower_left, lower_right], axis=1)
    return jnp.concatenate([top_rows, bottom_rows], axis=0)


def factor_split(diag_part):
    full_diag = lax.all_gather(diag_part, "row", axis=1, tiled=True)
    return block_cholesky(full_diag)


def local(edge_factor, mass, rhs):
    factor_rows = edge_factor[0]
    mass_rows = mass[0]
    rhs_cols = rhs[0]
    quarter = factor_rows.shape[0]
    node_count = factor_rows.shape[1]
    blocks = lax.axis_size("tm")
    at_start = lax.axis_index("tm") == 0
    edge_cols = jnp.dot(
        lax.all_gather(factor_rows, "row", axis=0, tiled=True),
        factor_rows.T,
        precision=exact_prec,
        preferred_element_type=jnp.float32,
    )
    edge_next = passed_along(edge_cols, "tm", -1)
    offset = lax.axis_index("row") * quarter
    row_ids = lax.broadcasted_iota(jnp.int32, (node_count, quarter), 0)
    col_ids = lax.broadcasted_iota(jnp.int32, (node_count, quarter), 1) + offset
    mass_diag = jnp.where(row_ids == col_ids, mass_rows[None, :], 0.0)
    diag_part = mass_diag + edge_cols + edge_next
    low_coupling = jnp.where(at_start, 0.0, -edge_cols)
    up_coupling = -edge_next
    stride = 1
    while stride < blocks:
        factor = factor_split(diag_part)
        whitened = solve_lower(
            factor, jnp.concatenate([low_coupling, up_coupling, rhs_cols], axis=1)
        )
        stacked = jnp.stack([whitened[:, :quarter], whitened[:, quarter : 2 * quarter]])
        gram_blocks = jnp.einsum(
            "tbn,bk->tnk",
            lax.all_gather(stacked, "row", axis=2, tiled=True),
            whitened,
            precision=exact_prec,
        )
        from_below = passed_along(gram_blocks[1], "tm", stride)
        from_above = passed_along(gram_blocks[0], "tm", -stride)
        diag_part = diag_part - from_below[:, quarter : 2 * quarter] - from_above[:, :quarter]
        low_coupling = -from_below[:, :quarter]
        up_coupling = -from_above[:, quarter : 2 * quarter]
        rhs_cols = rhs_cols - from_below[:, 2 * quarter :] - from_above[:, 2 * quarter :]
        stride = stride * 2
    factor = factor_split(diag_part)
    inner = solve_lower(factor, rhs_cols)
    solution = jax.scipy.linalg.solve_triangular(factor, inner, lower=True, trans=1)
    return solution[None]


def solution(mesh):
    placed = (P("tm", "row", None), P("tm", "row"), P("tm", None, "row"))
    return jax.shard_map(
        local, mesh=mesh, in_specs=placed, out_specs=P("tm", None, "row"), check_vma=False
    )
```

profile of v0, /device:TPU:0, one launch (start us, length us, event | category | flops | bytes accessed | tf_op | source)
XLA Modules:
  0.0 921.7 jit_solution(4415967617176737400)
XLA Ops:
  7.3 21.1 %all-gather.24.cloned.1.call-done = f32[1,512,512]{2,1,0:T(8,128)} async-done(((f32[1,128,512]{2,1,0:T(8,128)}), f32[1,512,512]{2,1,0:T(8,128)}) %all-gather.24.cloned.1.call-update) | async-done | bytes 1048592 | tf_op jit(solution)/shard_map/all_gather | solution.py:46
  28.4 2.5 fusion.4
  32.2 9.0 collective-permute-done
  41.2 1.5 add_add_fusion
  43.0 16.6 %all-gather.10.cloned.1.call-done = f32[512,512]{0,1:T(8,128)} async-done(((f32[512,128]{0,1:T(8,128)}), f32[512,512]{0,1:T(8,128)}) %all-gather.10.cloned.1.call-update) | async-done | bytes 1048592 | tf_op jit(solution)/shard_map/all_gather | solution.py:33
  61.7 11.7 %cholesky.382 = f32[128,128]{1,0:T(8,128)S(1)} custom-call(f32[128,128]{1,0:T(8,128)S(1)} %cholesky.650), custom_call_target="Cholesky" | custom-call | tf_op jit(solution)/shard_map/jit(cholesky)/cholesky | solution.py:21
  73.5 9.8 %custom-call.34 = f32[1,128,128]{1,2,0:T(8,128)S(1)} custom-call(f32[1,128,128]{2,1,0:T(8,128)S(1)} %get-tuple-element.213), custom_call_target="InvertDiagBlocksLowerTriangular" | custom-call | tf_op jit(solution)/shard_map/jit(cholesky)/cholesky | solution.py:21
  83.8 11.7 %cholesky.399 = f32[128,128]{1,0:T(8,128)S(1)} custom-call(f32[128,128]{1,0:T(8,128)S(1)} %convolution_subtract_fusion.9), custom_call_target="Cholesky" | custom-call | tf_op jit(solution)/shard_map/jit(cholesky)/cholesky | solution.py:21
  97.7 4.2 while.16
  101.9 19.7 %custom-call.35 = f32[2,128,128]{1,2,0:T(8,128)S(1)} custom-call(f32[2,128,128]{2,1,0:T(8,128)S(1)} %get-tuple-element.62), custom_call_target="InvertDiagBlocksLowerTriangular" | custom-call | tf_op jit(solution)/shard_map/jit(_solve_triangular)/triangular_solve | solution.py:16
  123.3 11.7 %cholesky.416 = f32[128,128]{1,0:T(8,128)S(1)} custom-call(f32[128,128]{1,0:T(8,128)S(1)} %cholesky.653), custom_call_target="Cholesky" | custom-call | tf_op jit(solution)/shard_map/jit(cholesky)/cholesky | solution.py:24
  135.1 9.8 %custom-call.36 = f32[1,128,128]{1,2,0:T(8,128)S(1)} custom-call(f32[1,128,128]{2,1,0:T(8,128)S(1)} %get-tuple-element.209), custom_call_target="InvertDiagBlocksLowerTriangular" | custom-call | tf_op jit(solution)/shard_map/jit(cholesky)/cholesky | solution.py:24
  145.6 11.7 %cholesky.433 = f32[128,128]{1,0:T(8,128)S(1)} custom-call(f32[128,128]{1,0:T(8,128)S(1)} %convolution_subtract_fusion.8), custom_call_target="Cholesky" | custom-call | tf_op jit(solution)/shard_map/jit(cholesky)/cholesky | solution.py:24
  160.2 8.1 while.17
  168.3 39.8 %custom-call.37 = f32[4,128,128]{1,2,0:T(8,128)S(1)} custom-call(f32[4,128,128]{2,1,0:T(8,128)S(1)} %get-tuple-element.63), custom_call_target="InvertDiagBlocksLowerTriangular" | custom-call | tf_op jit(solution)/shard_map/jit(_solve_triangular)/triangular_solve | solution.py:16
  213.2 22.9 %all-gather.12.cloned.1.call-done = f32[2,512,512]{2,1,0:T(8,128)} async-done(((f32[2,512,128]{2,1,0:T(8,128)}), f32[2,512,512]{2,1,0:T(8,128)}) %all-gather.12.cloned.1.call-update) | async-done | bytes 2097168 | tf_op jit(solution)/shard_map/all_gather | solution.py:68
  236.2 4.3 fusion.10
  240.6 3.4 collective-permute-start.1
  245.4 32.7 %collective-permute-done.1 = f32[512,384]{0,1:T(8,128)S(1)} collective-permute-done((f32[512,384]{0,1:T(8,128)S(1)}, f32[512,384]{0,1:T(8,128)S(1)}, u32[]{:S(2)}, u32[]{:S(2)}) %collective-permute-start.1) | collective-permute-done | bytes 786464 | tf_op jit(solution)/shard_map/ppermute | solution.py:12
  279.4 17.6 %all-gather.14.cloned.1.call-done = f32[512,512]{0,1:T(8,128)} async-done(((f32[512,128]{0,1:T(8,128)}), f32[512,512]{0,1:T(8,128)}) %all-gather.14.cloned.1.call-update) | async-done | bytes 1048592 | tf_op jit(solution)/shard_map/all_gather | solution.py:33
  299.1 11.7 %cholesky.450 = f32[128,128]{1,0:T(8,128)S(1)} custom-call(f32[128,128]{1,0:T(8,128)S(1)} %cholesky.656), custom_call_target="Cholesky" | custom-call | tf_op jit(solution)/shard_map/jit(cholesky)/cholesky | solution.py:21
  310.9 9.8 %custom-call.38 = f32[1,128,128]{1,2,0:T(8,128)S(1)} custom-call(f32[1,128,128]{2,1,0:T(8,128)S(1)} %get-tuple-element.205), custom_call_target="InvertDiagBlocksLowerTriangular" | custom-call | tf_op jit(solution)/shard_map/jit(cholesky)/cholesky | solution.py:21
  321.2 11.7 %cholesky.467 = f32[128,128]{1,0:T(8,128)S(1)} custom-call(f32[128,128]{1,0:T(8,128)S(1)} %convolution_subtract_fusion.7), custom_call_target="Cholesky" | custom-call | tf_op jit(solution)/shard_map/jit(cholesky)/cholesky | solution.py:21
  335.7 4.0 while.18
  339.7 19.9 %custom-call.39 = f32[2,128,128]{1,2,0:T(8,128)S(1)} custom-call(f32[2,128,128]{2,1,0:T(8,128)S(1)} %get-tuple-element.64), custom_call_target="InvertDiagBlocksLowerTriangular" | custom-call | tf_op jit(solution)/shard_map/jit(_solve_triangular)/triangular_solve | solution.py:16
  361.3 11.7 %cholesky.484 = f32[128,128]{1,0:T(8,128)S(1)} custom-call(f32[128,128]{1,0:T(8,128)S(1)} %cholesky.659), custom_call_target="Cholesky" | custom-call | tf_op jit(solution)/shard_map/jit(cholesky)/cholesky | solution.py:24
  373.1 9.8 %custom-call.40 = f32[1,128,128]{1,2,0:T(8,128)S(1)} custom-call(f32[1,128,128]{2,1,0:T(8,128)S(1)} %get-tuple-element.201), custom_call_target="InvertDiagBlocksLowerTriangular" | custom-call | tf_op jit(solution)/shard_map/jit(cholesky)/cholesky | solution.py:24
  383.6 11.7 %cholesky.501 = f32[128,128]{1,0:T(8,128)S(1)} custom-call(f32[128,128]{1,0:T(8,128)S(1)} %convolution_subtract_fusion.6), custom_call_target="Cholesky" | custom-call | tf_op jit(solution)/shard_map/jit(cholesky)/cholesky | solution.py:24
  398.1 8.1 while.19
  406.3 39.7 %custom-call.41 = f32[4,128,128]{1,2,0:T(8,128)S(1)} custom-call(f32[4,128,128]{2,1,0:T(8,128)S(1)} %get-tuple-element.65), custom_call_target="InvertDiagBlocksLowerTriangular" | custom-call | tf_op jit(solution)/shard_map/jit(_solve_triangular)/triangular_solve | solution.py:16
  451.1 22.9 %all-gather.16.cloned.1.call-done = f32[2,512,512]{2,1,0:T(8,128)} async-done(((f32[2,512,128]{2,1,0:T(8,128)}), f32[2,512,512]{2,1,0:T(8,128)}) %all-gather.16.cloned.1.call-update) | async-done | bytes 2097168 | tf_op jit(solution)/shard_map/all_gather | solution.py:68
  474.1 4.3 fusion.8
  478.6 3.4 collective-permute-start.3
  483.3 15.9 %collective-permute-done.3 = f32[512,384]{0,1:T(8,128)S(1)} collective-permute-done((f32[512,384]{0,1:T(8,128)S(1)}, f32[512,384]{0,1:T(8,128)S(1)}, u32[]{:S(2)}, u32[]{:S(2)}) %collective-permute-start.3) | collective-permute-done | bytes 786464 | tf_op jit(solution)/shard_map/ppermute | solution.py:12
  499.2 4.2 collective-permute-done.4
  504.6 15.6 %all-gather.18.cloned.1.call-done = f32[512,512]{0,1:T(8,128)} async-done(((f32[512,128]{0,1:T(8,128)}), f32[512,512]{0,1:T(8,128)}) %all-gather.18.cloned.1.call-update) | async-done | bytes 1048592 | tf_op jit(solution)/shard_map/all_gather | solution.py:33
  522.4 11.7 %cholesky.518 = f32[128,128]{1,0:T(8,128)S(1)} custom-call(f32[128,128]{1,0:T(8,128)S(1)} %cholesky.662), custom_call_target="Cholesky" | custom-call | tf_op jit(solution)/shard_map/jit(cholesky)/cholesky | solution.py:21
  534.2 9.8 %custom-call.42 = f32[1,128,128]{1,2,0:T(8,128)S(1)} custom-call(f32[1,128,128]{2,1,0:T(8,128)S(1)} %get-tuple-element.197), custom_call_target="InvertDiagBlocksLowerTriangular" | custom-call | tf_op jit(solution)/shard_map/jit(cholesky)/cholesky | solution.py:21
  544.5 11.7 %cholesky.535 = f32[128,128]{1,0:T(8,128)S(1)} custom-call(f32[128,128]{1,0:T(8,128)S(1)} %convolution_subtract_fusion.5), custom_call_target="Cholesky" | custom-call | tf_op jit(solution)/shard_map/jit(cholesky)/cholesky | solution.py:21
  558.9 4.0 while.20
  562.9 19.9 %custom-call.43 = f32[2,128,128]{1,2,0:T(8,128)S(1)} custom-call(f32[2,128,128]{2,1,0:T(8,128)S(1)} %get-tuple-element.66), custom_call_target="InvertDiagBlocksLowerTriangular" | custom-call | tf_op jit(solution)/shard_map/jit(_solve_triangular)/triangular_solve | solution.py:16
  584.6 11.7 %cholesky.552 = f32[128,128]{1,0:T(8,128)S(1)} custom-call(f32[128,128]{1,0:T(8,128)S(1)} %cholesky.665), custom_call_target="Cholesky" | custom-call | tf_op jit(solution)/shard_map/jit(cholesky)/cholesky | solution.py:24
  596.3 9.8 %custom-call.44 = f32[1,128,128]{1,2,0:T(8,128)S(1)} custom-call(f32[1,128,128]{2,1,0:T(8,128)S(1)} %get-tuple-element.193), custom_call_target="InvertDiagBlocksLowerTriangular" | custom-call | tf_op jit(solution)/shard_map/jit(cholesky)/cholesky | solution.py:24
  606.9 11.7 %cholesky.569 = f32[128,128]{1,0:T(8,128)S(1)} custom-call(f32[128,128]{1,0:T(8,128)S(1)} %convolution_subtract_fusion.4), custom_call_target="Cholesky" | custom-call | tf_op jit(solution)/shard_map/jit(cholesky)/cholesky | solution.py:24
  621.4 8.1 while.21
  629.6 39.7 %custom-call.45 = f32[4,128,128]{1,2,0:T(8,128)S(1)} custom-call(f32[4,128,128]{2,1,0:T(8,128)S(1)} %get-tuple-element.67), custom_call_target="InvertDiagBlocksLowerTriangular" | custom-call | tf_op jit(solution)/shard_map/jit(_solve_triangular)/triangular_solve | solution.py:16
  674.4 22.9 %all-gather.20.cloned.1.call-done = f32[2,512,512]{2,1,0:T(8,128)} async-done(((f32[2,512,128]{2,1,0:T(8,128)}), f32[2,512,512]{2,1,0:T(8,128)}) %all-gather.20.cloned.1.call-update) | async-done | bytes 2097168 | tf_op jit(solution)/shard_map/all_gather | solution.py:68
  697.4 4.3 fusion.6
  701.8 4.4 collective-permute-start.5
  706.2 1.5 collective-permute-start.6
  707.7 15.7 %collective-permute-done.5 = f32[512,384]{0,1:T(8,128)S(1)} collective-permute-done((f32[512,384]{0,1:T(8,128)S(1)}, f32[512,384]{0,1:T(8,128)S(1)}, u32[]{:S(2)}, u32[]{:S(2)}) %collective-permute-start.5) | collective-permute-done | bytes 786464 | tf_op jit(solution)/shard_map/ppermute | solution.py:12
  723.4 21.9 %collective-permute-done.6 = f32[512,384]{0,1:T(8,128)S(1)} collective-permute-done((f32[512,384]{0,1:T(8,128)S(1)}, f32[512,384]{0,1:T(8,128)S(1)}, u32[]{:S(2)}, u32[]{:S(2)}) %collective-permute-start.6) | collective-permute-done | bytes 786464 | tf_op jit(solution)/shard_map/ppermute | solution.py:12
  746.1 14.1 %all-gather.22.cloned.1.call-done = f32[512,512]{0,1:T(8,128)} async-done(((f32[512,128]{0,1:T(8,128)}), f32[512,512]{0,1:T(8,128)}) %all-gather.22.cloned.1.call-update) | async-done | bytes 1048592 | tf_op jit(solution)/shard_map/all_gather | solution.py:33
  762.5 11.7 %cholesky.586 = f32[128,128]{1,0:T(8,128)S(1)} custom-call(f32[128,128]{1,0:T(8,128)S(1)} %cholesky.668), custom_call_target="Cholesky" | custom-call | tf_op jit(solution)/shard_map/jit(cholesky)/cholesky | solution.py:21
  774.2 9.8 %custom-call.46 = f32[1,128,128]{1,2,0:T(8,128)S(1)} custom-call(f32[1,128,128]{2,1,0:T(8,128)S(1)} %get-tuple-element.189), custom_call_target="InvertDiagBlocksLowerTriangular" | custom-call | tf_op jit(solution)/shard_map/jit(cholesky)/cholesky | solution.py:21
  784.5 11.7 %cholesky.603 = f32[128,128]{1,0:T(8,128)S(1)} custom-call(f32[128,128]{1,0:T(8,128)S(1)} %convolution_subtract_fusion.3), custom_call_target="Cholesky" | custom-call | tf_op jit(solution)/shard_map/jit(cholesky)/cholesky | solution.py:21
  798.8 3.8 while.22
  802.7 19.9 %custom-call.47 = f32[2,128,128]{1,2,0:T(8,128)S(1)} custom-call(f32[2,128,128]{2,1,0:T(8,128)S(1)} %get-tuple-element.68), custom_call_target="InvertDiagBlocksLowerTriangular" | custom-call | tf_op jit(solution)/shard_map/jit(_solve_triangular)/triangular_solve | solution.py:16
  824.3 11.7 %cholesky.620 = f32[128,128]{1,0:T(8,128)S(1)} custom-call(f32[128,128]{1,0:T(8,128)S(1)} %cholesky.671), custom_call_target="Cholesky" | custom-call | tf_op jit(solution)/shard_map/jit(cholesky)/cholesky | solution.py:24
  836.1 9.8 %custom-call.48 = f32[1,128,128]{1,2,0:T(8,128)S(1)} custom-call(f32[1,128,128]{2,1,0:T(8,128)S(1)} %get-tuple-element.185), custom_call_target="InvertDiagBlocksLowerTriangular" | custom-call | tf_op jit(solution)/shard_map/jit(cholesky)/cholesky | solution.py:24
  846.6 11.7 %cholesky.637 = f32[128,128]{1,0:T(8,128)S(1)} custom-call(f32[128,128]{1,0:T(8,128)S(1)} %convolution_subtract_fusion.2), custom_call_target="Cholesky" | custom-call | tf_op jit(solution)/shard_map/jit(cholesky)/cholesky | solution.py:24
  861.2 8.5 while.15
  861.9 1.4 bitcast_dynamic-update-slice_fusion.16
  869.7 39.6 %custom-call.21 = f32[4,128,128]{1,2,0:T(8,128)S(1)} custom-call(f32[4,128,128]{2,1,0:T(8,128)S(1)} %get-tuple-element.31), custom_call_target="InvertDiagBlocksLowerTriangular" | custom-call | tf_op jit(solution)/shard_map/jit(_solve_triangular)/triangular_solve | solution.py:81
  (302 shorter events, 107.1 us)
Async XLA Ops:
  6.5 36.2 %copy-start.7 = (f32[1,512,128]{2,1,0:T(8,128)S(1)}, f32[1,512,128]{2,1,0:T(8,128)}, u32[]{:S(2)}) copy-start(f32[1,512,128]{2,1,0:T(8,128)} %param.10) | copy-start | bytes 786436
  6.5 21.8 %all-gather.24.cloned.1.call-start = ((), (), s32[]{:S(2)}) async-start(), calls=%async_computation.7 | async-start | bytes 1310720 | tf_op jit(solution)/shard_map/all_gather | solution.py:46
  7.3 52.3 %all-gather.10.cloned.1.call-start = ((), (), s32[]{:S(2)}) async-start(), calls=%async_computation | async-start | bytes 1310720 | tf_op jit(solution)/shard_map/all_gather | solution.py:33
  30.8 10.3 %collective-permute-start = (f32[512,128]{0,1:T(8,128)S(1)}, f32[512,128]{0,1:T(8,128)S(1)}, u32[]{:S(2)}, u32[]{:S(2)}) collective-permute-start(f32[512,128]{0,1:T(8,128)S(1)} %fusion.4), channel_id=1, source_target_pairs={{4,0},{8,4},{12,8},{16,12},{20,16},{24,20},{28,24},{5,1},{9,5},{13... | collective-permute-start | bytes 786440 | tf_op jit(solution)/shard_map/ppermute | solution.py:12
  42.7 193.5 %all-gather.12.cloned.1.call-start = ((), (), s32[]{:S(2)}) async-start(), calls=%async_computation.1 | async-start | bytes 2621440 | tf_op jit(solution)/shard_map/all_gather | solution.py:68
  60.5 61.1 %copy-start.3 = (f32[512,512]{0,1:T(8,128)S(1)}, f32[512,512]{0,1:T(8,128)}, u32[]{:S(2)}) copy-start(f32[512,512]{0,1:T(8,128)} %all-gather.10.cloned.1.call-done) | copy-start | bytes 3145732
  213.2 83.8 %all-gather.14.cloned.1.call-start = ((), (), s32[]{:S(2)}) async-start(), calls=%async_computation.2 | async-start | bytes 1310720 | tf_op jit(solution)/shard_map/all_gather | solution.py:33
  240.5 37.6 %copy-start.1 = (f32[512,128]{0,1:T(8,128)S(1)}, f32[512,128]{0,1:T(8,128)}, u32[]{:S(2)}) copy-start(f32[512,128]{0,1:T(8,128)} %get-tuple-element.179) | copy-start | bytes 786436
  240.6 37.4 %collective-permute-start.1 = (f32[512,384]{0,1:T(8,128)S(1)}, f32[512,384]{0,1:T(8,128)S(1)}, u32[]{:S(2)}, u32[]{:S(2)}) collective-permute-start(f32[512,384]{0,1:T(8,128)S(1)} %get-tuple-element.167), channel_id=1, source_target_pairs={{0,4},{4,8},{8,12},{12,16},{16,20},{20,24},{24,28},{1,5},{5,9},{9,... | collective-permute-start | bytes 2359304 | tf_op jit(solution)/shard_map/ppermute | solution.py:12
  244.1 34.0 %collective-permute-start.2 = (f32[512,384]{0,1:T(8,128)S(1)}, f32[512,384]{0,1:T(8,128)S(1)}, u32[]{:S(2)}, u32[]{:S(2)}) collective-permute-start(f32[512,384]{0,1:T(8,128)S(1)} %get-tuple-element.168), channel_id=1, source_target_pairs={{4,0},{8,4},{12,8},{16,12},{20,16},{24,20},{28,24},{5,1},{9,5},{13... | collective-permute-start | bytes 2359304 | tf_op jit(solution)/shard_map/ppermute | solution.py:12
  279.1 195.0 %all-gather.16.cloned.1.call-start = ((), (), s32[]{:S(2)}) async-start(), calls=%async_computation.3 | async-start | bytes 2621440 | tf_op jit(solution)/shard_map/all_gather | solution.py:68
  297.9 61.6 %copy-start.4 = (f32[512,512]{0,1:T(8,128)S(1)}, f32[512,512]{0,1:T(8,128)}, u32[]{:S(2)}) copy-start(f32[512,512]{0,1:T(8,128)} %all-gather.14.cloned.1.call-done) | copy-start | bytes 3145732
  451.1 69.1 %all-gather.18.cloned.1.call-start = ((), (), s32[]{:S(2)}) async-start(), calls=%async_computation.4 | async-start | bytes 1310720 | tf_op jit(solution)/shard_map/all_gather | solution.py:33
  478.4 24.9 %copy-start = (f32[512,128]{0,1:T(8,128)S(1)}, f32[512,128]{0,1:T(8,128)}, u32[]{:S(2)}) copy-start(f32[512,128]{0,1:T(8,128)} %get-tuple-element.165) | copy-start | bytes 786436
  478.6 20.6 %collective-permute-start.3 = (f32[512,384]{0,1:T(8,128)S(1)}, f32[512,384]{0,1:T(8,128)S(1)}, u32[]{:S(2)}, u32[]{:S(2)}) collective-permute-start(f32[512,384]{0,1:T(8,128)S(1)} %get-tuple-element.163), channel_id=1, source_target_pairs={{0,8},{4,12},{8,16},{12,20},{16,24},{20,28},{1,9},{5,13},{9,17},{1... | collective-permute-start | bytes 2359304 | tf_op jit(solution)/shard_map/ppermute | solution.py:12
  482.0 21.3 %collective-permute-start.4 = (f32[512,384]{0,1:T(8,128)S(1)}, f32[512,384]{0,1:T(8,128)S(1)}, u32[]{:S(2)}, u32[]{:S(2)}) collective-permute-start(f32[512,384]{0,1:T(8,128)S(1)} %get-tuple-element.164), channel_id=1, source_target_pairs={{8,0},{12,4},{16,8},{20,12},{24,16},{28,20},{9,1},{13,5},{17,9},{2... | collective-permute-start | bytes 2359304 | tf_op jit(solution)/shard_map/ppermute | solution.py:12
  504.3 193.1 %all-gather.20.cloned.1.call-start = ((), (), s32[]{:S(2)}) async-start(), calls=%async_computation.5 | async-start | bytes 2621440 | tf_op jit(solution)/shard_map/all_gather | solution.py:68
  521.2 61.6 %copy-start.5 = (f32[512,512]{0,1:T(8,128)S(1)}, f32[512,512]{0,1:T(8,128)}, u32[]{:S(2)}) copy-start(f32[512,512]{0,1:T(8,128)} %all-gather.18.cloned.1.call-done) | copy-start | bytes 3145732
  674.4 85.9 %all-gather.22.cloned.1.call-start = ((), (), s32[]{:S(2)}) async-start(), calls=%async_computation.6 | async-start | bytes 1310720 | tf_op jit(solution)/shard_map/all_gather | solution.py:33
  701.7 43.6 %copy-start.2 = (f32[512,128]{0,1:T(8,128)S(1)}, f32[512,128]{0,1:T(8,128)}, u32[]{:S(2)}) copy-start(f32[512,128]{0,1:T(8,128)} %get-tuple-element.161) | copy-start | bytes 786436
  701.8 21.6 %collective-permute-start.5 = (f32[512,384]{0,1:T(8,128)S(1)}, f32[512,384]{0,1:T(8,128)S(1)}, u32[]{:S(2)}, u32[]{:S(2)}) collective-permute-start(f32[512,384]{0,1:T(8,128)S(1)} %get-tuple-element.159), channel_id=1, source_target_pairs={{0,16},{4,20},{8,24},{12,28},{1,17},{5,21},{9,25},{13,29},{2,18},{... | collective-permute-start | bytes 2359304 | tf_op jit(solution)/shard_map/ppermute | solution.py:12
  706.2 39.1 %collective-permute-start.6 = (f32[512,384]{0,1:T(8,128)S(1)}, f32[512,384]{0,1:T(8,128)S(1)}, u32[]{:S(2)}, u32[]{:S(2)}) collective-permute-start(f32[512,384]{0,1:T(8,128)S(1)} %get-tuple-element.160), channel_id=1, source_target_pairs={{16,0},{20,4},{24,8},{28,12},{17,1},{21,5},{25,9},{29,13},{18,2},{... | collective-permute-start | bytes 2359304 | tf_op jit(solution)/shard_map/ppermute | solution.py:12
  761.2 61.3 %copy-start.6 = (f32[512,512]{0,1:T(8,128)S(1)}, f32[512,512]{0,1:T(8,128)}, u32[]{:S(2)}) copy-start(f32[512,512]{0,1:T(8,128)} %all-gather.22.cloned.1.call-done) | copy-start | bytes 3145732
Sparse Core Ops, SparseCore 0:
  8.9 19.4 all-gather.23
  42.8 16.6 all-gather.9
  213.3 22.8 all-gather.11
  279.2 17.7 all-gather.13
  451.2 22.8 all-gather.15
  504.4 15.7 all-gather.17
  674.5 22.8 all-gather.19
  746.3 13.9 all-gather.21
where the time goes:
time: 931 us; the launch traced here: 922 us
  other arithmetic  528 us (57%)
  waiting for transfers between devices  254 us (27%)
  local copies, waits for them, and re-layouts  54.8 us (6%)
  matrix products  41.6 us (4%)
  between operations  25.6 us (3%)
  starting transfers between devices  17.2 us (2%)
    another operation x19, other arithmetic, solve_lower(): return jax.scipy.linalg.solve_triangular(factor, values, lower=True)  199 us
    another operation x28, other arithmetic, block_cholesky(): lower_right = jnp.linalg.cholesky(schur_part)  139 us
    another operation x27, other arithmetic, block_cholesky(): upper_left = jnp.linalg.cholesky(matrix[:half, :half])  138 us
    ppermute x7, waiting for transfers between devices, passed_along(): return lax.ppermute(block, axis, route)  99.3 us
    all_gather x3, waiting for transfers between devices, local(): lax.all_gather(stacked, 'row', axis=2, tiled=True)  68.8 us
    all_gather x4, waiting for transfers between devices, factor_split(): full_diag = lax.all_gather(diag_part, 'row', axis=1, tiled=True)  63.9 us
    another operation x74, local copies, waits for them, and re-layouts, solve_lower(): return jax.scipy.linalg.solve_triangular(factor, values, lower=True)  40.3 us
    another operation x2, other arithmetic, local(): jax.scipy.linalg.solve_triangular(factor, inner, lower=True, trans=1)  39.7 us
  transfers between devices with their start and end apart: 15, of which 14 were waited for; matrix products, arithmetic and copies ran while one was open for 0% of the time, Pallas kernels for 0%

commit v1 on v0

v1 whole, which is shorter than its diff:
```python
import functools

import jax
import jax.numpy as jnp
from jax import lax
from jax.experimental import pallas as pl
from jax.experimental.pallas import tpu as pltpu
from jax.sharding import PartitionSpec as P

exact_prec = lax.Precision.HIGHEST
lanes = 128
group = 8
vmem_bytes = 58 * 1024 * 1024


def dot(a, b):
    return lax.dot_general(
        a, b, (((1,), (0,)), ((), ())), precision=exact_prec, preferred_element_type=jnp.float32
    )


def dot_nt(a, b):
    return lax.dot_general(
        a, b, (((1,), (1,)), ((), ())), precision=exact_prec, preferred_element_type=jnp.float32
    )


def spread_rows(row):
    return jnp.broadcast_to(row, (group, lanes))


def inverse_8(cols, sub_ids):
    for k in range(0, group, 2):
        u, v = cols[k], cols[k + 1]
        a = spread_rows(u[k : k + 1])
        b = spread_rows(u[k + 1 : k + 2])
        c = spread_rows(v[k + 1 : k + 2])
        scale = 1.0 / (a * c - b * b)
        inv_a, inv_b, inv_c = c * scale, -b * scale, a * scale
        is_k, is_l = sub_ids == k, sub_ids == k + 1
        pair = is_k | is_l
        first = jnp.where(is_k, inv_a, jnp.where(is_l, inv_b, -(inv_a * u + inv_b * v)))
        second = jnp.where(is_k, inv_b, jnp.where(is_l, inv_c, -(inv_b * u + inv_c * v)))
        done = []
        for j in range(group):
            if j == k:
                done.append(first)
            elif j == k + 1:
                done.append(second)
            else:
                row_k = spread_rows(cols[j][k : k + 1])
                row_l = spread_rows(cols[j][k + 1 : k + 2])
                kept = jnp.where(pair, 0.0, cols[j])
                done.append(kept + (first * row_k + second * row_l))
        cols = done
    return cols


def inverse_128(block):
    slabs = [block[group * i : group * (i + 1)] for i in range(lanes // group)]
    sub_ids = lax.broadcasted_iota(jnp.int32, (group, lanes), 0)
    lane_ids = lax.broadcasted_iota(jnp.int32, (group, lanes), 1)
    for p in range(lanes // group):
        start = group * p
        own = (lane_ids >= start) & (lane_ids < start + group)
        unit = jnp.where(lane_ids == sub_ids + start, 1.0, 0.0)
        spread = lambda slab, j: jnp.broadcast_to(
            slab[:, start + j : start + j + 1], (group, lanes)
        )
        small = inverse_8([spread(slabs[p], j) for j in range(group)], sub_ids)
        pivot = jnp.where(own, unit, slabs[p])
        solved = small[0] * spread_rows(pivot[0:1])
        for j in range(1, group):
            solved = solved + small[j] * spread_rows(pivot[j : j + 1])
        solved_rows = [spread_rows(solved[j : j + 1]) for j in range(group)]
        done = []
        for i in range(lanes // group):
            if i == p:
                done.append(solved)
                continue
            change = spread(slabs[i], 0) * solved_rows[0]
            for j in range(1, group):
                change = change + spread(slabs[i], j) * solved_rows[j]
            done.append(jnp.where(own, 0.0, slabs[i]) - change)
        slabs = done
    return jnp.concatenate(slabs, axis=0)


def eliminate(table, size):
    panels = size // lanes
    for p in range(panels):
        at, after = lanes * p, lanes * (p + 1)
        inverse = inverse_128(table[at:after, at:after])
        solved = dot(inverse, table[at:after, after:])
        for q in range(panels):
            if q != p:
                rows = slice(lanes * q, lanes * (q + 1))
                table[rows, after:] = table[rows, after:] - dot(table[rows, at:after], solved)
        table[at:after, after:] = solved


def add_mass(table, gathered, block, size):
    quarter = gathered.shape[2] - group
    for s in range(size // quarter):
        rows = slice(quarter * s, quarter * (s + 1))
        mass = gathered[block, s, quarter : quarter + 1, :quarter]
        ids = (quarter, quarter)
        diag = lax.broadcasted_iota(jnp.int32, ids, 0) == lax.broadcasted_iota(jnp.int32, ids, 1)
        table[rows, rows] = table[rows, rows] + jnp.where(diag, mass, 0.0)


def factor_of(gathered, block, size):
    quarter = gathered.shape[2] - group
    return jnp.concatenate([gathered[block, s, :quarter, :] for s in range(size // quarter)], axis=0)


def chain_kernel(steps, side_ref, gathered, rhs, solved, carry, last_edge, table):
    size = table.shape[0]
    right = side_ref[0]
    start = factor_of(gathered, 0, size)
    start_gram = dot_nt(start, start)
    last_edge[...] = jnp.where(right == 0, start_gram, 0.0)
    carry[...] = jnp.zeros_like(carry)

    def step(i, _):
        block = jnp.where(right == 0, i, steps - i)
        edge_block = jnp.where(right == 0, i + 1, steps - i)
        factor = factor_of(gathered, edge_block, size)
        edge = dot_nt(factor, factor)
        table[:, :size] = last_edge[...] + edge - carry[:, :size]
        add_mass(table, gathered, block, size)
        table[:, size : 2 * size] = edge
        table[:, 2 * size :] = rhs[block] + carry[:, size:]
        last_edge[...] = edge
        eliminate(table, size)
        solved[i] = table[:, size:]
        carry[...] = dot(last_edge[...], table[:, size:])
        return 0

    lax.fori_loop(0, steps, step, 0)


def middle_kernel(steps, side_ref, gathered, from_right, rhs, carry, last_edge, reduced, sent, table, kept):
    size = table.shape[0]
    right = side_ref[0]
    block = jnp.where(right == 0, steps, 0)

    @pl.when(right == 0)
    def _():
        factor = factor_of(from_right, 0, size)
        table[:, size : 2 * size] = dot_nt(factor, factor)

    @pl.when(right != 0)
    def _():
        factor = factor_of(gathered, 0, size)
        table[:, size : 2 * size] = dot_nt(factor, factor)

    edge = table[:, size : 2 * size]
    table[:, :size] = last_edge[...] + edge - carry[:, :size]
    add_mass(table, gathered, block, size)
    table[:, 2 * size :] = rhs[block] + carry[:, size:]
    reduced[:, :size] = table[:, :size]
    reduced[:, size:] = table[:, 2 * size :]
    kept[...] = edge
    eliminate(table, size)
    sent[...] = dot(kept[...], table[:, size:])


def final_kernel(steps, side_ref, reduced, received, solved, out, table):
    size = table.shape[0]
    place = side_ref[1]
    table[:, :size] = reduced[:, :size] - received[:, :size]
    table[:, size:] = reduced[:, size:] + received[:, size:]
    eliminate(table, size)

    @pl.when(place == steps)
    def _():
        out[...] = table[:, size:]

    def back(n, _):
        i = steps - 1 - n
        here = solved[i, :, size:] + dot(solved[i, :, :size], table[:, size:])
        table[:, size:] = here

        @pl.when(place == i)
        def _():
            out[...] = here

        return 0

    lax.fori_loop(0, steps, back, 0)


def local(edge_factor, mass, rhs):
    _, quarter, size = edge_factor.shape
    cols = rhs.shape[2]
    blocks, parts = lax.axis_size("tm"), lax.axis_size("row")
    half = blocks // 2
    steps = half - 1
    mine = lax.axis_index("tm")
    right = (mine >= half).astype(jnp.int32)
    place = jnp.where(right == 0, mine, blocks - 1 - mine)
    side = jnp.stack([right, place]).astype(jnp.int32)

    halves = [[side_at * half + i for i in range(half)] for side_at in range(2)]
    halves_all = [[t * parts + r for t in ids for r in range(parts)] for ids in halves]
    mass_rows = jnp.pad(mass, ((0, group - 1), (0, size - quarter)))
    packed = jnp.concatenate([edge_factor[0], mass_rows], axis=0)
    gathered = lax.all_gather(packed, ("tm", "row"), axis_index_groups=halves_all)
    gathered = gathered.reshape(half, parts, quarter + group, size)
    rhs_half = lax.all_gather(rhs[0], "tm", axis_index_groups=halves)
    down = [(t + half, t) for t in range(half)]
    from_right = lax.ppermute(gathered[:1], "tm", down)

    smem = pl.BlockSpec(memory_space=pltpu.SMEM)
    vmem = pl.BlockSpec(memory_space=pltpu.VMEM)
    params = pltpu.CompilerParams(vmem_limit_bytes=vmem_bytes)
    f32 = lambda *shape: jax.ShapeDtypeStruct(shape, jnp.float32)
    scratch = lambda *shape: pltpu.VMEM(shape, jnp.float32)

    solved, carry, last_edge = pl.pallas_call(
        functools.partial(chain_kernel, steps),
        out_shape=(f32(steps, size, size + cols), f32(size, size + cols), f32(size, size)),
        in_specs=[smem, vmem, vmem],
        out_specs=(vmem, vmem, vmem),
        scratch_shapes=[scratch(size, 2 * size + cols)],
        compiler_params=params,
    )(side, gathered, rhs_half)

    reduced, sent = pl.pallas_call(
        functools.partial(middle_kernel, steps),
        out_shape=(f32(size, size + cols), f32(size, size + cols)),
        in_specs=[smem] + [vmem] * 5,
        out_specs=(vmem, vmem),
        scratch_shapes=[scratch(size, 2 * size + cols), scratch(size, size)],
        compiler_params=params,
    )(side, gathered, from_right, rhs_half, carry, last_edge)

    across = [(t, (t + half) % blocks) for t in range(blocks)]
    received = lax.ppermute(sent, "tm", across)

    solution = pl.pallas_call(
        functools.partial(final_kernel, steps),
        out_shape=f32(size, cols),
        in_specs=[smem] + [vmem] * 3,
        out_specs=vmem,
        scratch_shapes=[scratch(size, size + cols)],
        compiler_params=params,
    )(side, reduced, received, solved)
    return solution[None]


def solution(mesh):
    placed = (P("tm", "row", None), P("tm", "row"), P("tm", None, "row"))
    return jax.shard_map(
        local, mesh=mesh, in_specs=placed, out_specs=P("tm", None, "row"), check_vma=False
    )
```

time: 931 us -> 325 us (0.35); the launches traced: 922 us -> 331 us
  other arithmetic: 528 us -> 2.31 us
  Pallas kernels: 0 us -> 187 us
  waiting for transfers between devices: 254 us -> 121 us
  local copies, waits for them, and re-layouts: 54.8 us -> 3.48 us
  matrix products: 41.6 us -> 0 us
  starting transfers between devices: 17.2 us -> 4.36 us
  between operations: 25.6 us -> 13.6 us
    another operation x79 -> x1, other arithmetic: 518 us -> 0.61 us  [local(): side = jnp.stack([right, place]).astype(jnp.int32)]
    pallas_call x0 -> x3, Pallas kernels: none -> 187 us  [the longest x1 122 us: local(): pl.pallas_call(functools.partial(chain_kernel, steps), out_shape=(f32(ste...]
    all_gather x8 -> x2, waiting for transfers between devices: 154 us -> 62.8 us  [the longest x1 37.9 us: local(): lax.all_gather(packed, ('tm', 'row'), axis_index_groups=halves_all)]
    another operation x113 -> x0, local copies, waits for them, and re-layouts: 49.4 us -> none  [the longest x74 40.3 us: solve_lower(): return jax.scipy.linalg.solve_triangular(factor, values, lower=True)]
    ppermute x7 -> x2, waiting for transfers between devices: 99.3 us -> 57.2 us  [the longest x1 57.1 us: local(): received = lax.ppermute(sent, 'tm', across)]
    another operation x63 -> x0, matrix products: 24.5 us -> none  [the longest x40 18.3 us: solve_lower(): return jax.scipy.linalg.solve_triangular(factor, values, lower=True)]
    dot_general x8 -> x0, matrix products: 17.1 us -> none  [the longest x3 13 us: local(): jnp.einsum('tbn,bk->tnk', lax.all_gather(stacked, 'row', axis=2, tiled=Tr...]
    ppermute x7 -> x2, starting transfers between devices: 16.6 us -> 4.32 us  [the longest x1 3.03 us: local(): received = lax.ppermute(sent, 'tm', across)]
  transfers between devices with their start and end apart: 15 -> 4, of which waited for: 14 -> 3; matrix products, arithmetic and copies ran while one was open for 0% -> 1% of each run, Pallas kernels for 0% -> 37%
where the time goes in v1:
time: 325 us; the launch traced here: 331 us
  Pallas kernels  187 us (58%)
  waiting for transfers between devices  121 us (37%)
  between operations  13.6 us (4%)
  starting transfers between devices  4.36 us (1%)
  local copies, waits for them, and re-layouts  3.48 us (1%)
    pallas_call x1, Pallas kernels, local(): pl.pallas_call(functools.partial(chain_kernel, steps), out_shape=(f32(ste...  122 us
    ppermute x1, waiting for transfers between devices, local(): received = lax.ppermute(sent, 'tm', across)  57.1 us
    all_gather x1, waiting for transfers between devices, local(): lax.all_gather(packed, ('tm', 'row'), axis_index_groups=halves_all)  37.9 us
    pallas_call x1, Pallas kernels, local(): pl.pallas_call(functools.partial(middle_kernel, steps), out_shape=(f32(si...  37.6 us
    pallas_call x1, Pallas kernels, local(): pl.pallas_call(functools.partial(final_kernel, steps), out_shape=f32(size...  27.1 us
    all_gather x1, waiting for transfers between devices, local(): rhs_half = lax.all_gather(rhs[0], 'tm', axis_index_groups=halves)  25 us
  transfers between devices with their start and end apart: 4, of which 3 were waited for; matrix products, arithmetic and copies ran while one was open for 1% of the time, Pallas kernels for 37%

profile of v1, /device:TPU:0, one launch (start us, length us, event | category | flops | bytes accessed | tf_op | source)
XLA Modules:
  0.0 331.4 jit_solution(8569832819932129980)
XLA Ops:
  6.5 0.0 all-gather.6.cloned.1.call-start
  6.5 1.7 select_maximum_fusion
  8.2 0.0 all-gather.6.cloned.1.call-update
  8.3 0.0 all-gather.4.cloned.1.call-start
  8.3 0.7 all-gather.4.cloned.1.call-update
  9.0 37.9 %all-gather.6.cloned.1.call-done = f32[2176,512]{1,0:T(8,128)} async-done(((f32[136,512]{1,0:T(8,128)}), f32[2176,512]{1,0:T(8,128)}) %all-gather.6.cloned.1.call-update) | async-done | bytes 4456464 | tf_op jit(solution)/shard_map/all_gather | solution.py:209
  46.9 1.3 slice.9
  48.2 1.3 collective-permute-start
  49.5 0.6 pad_add_fusion.side_ref
  50.1 25.0 %all-gather.4.cloned.1.call-done.rhs = f32[4,512,128]{2,1,0:T(8,128)} async-done(((f32[1,512,128]{2,1,0:T(8,128)}), f32[4,512,128]{2,1,0:T(8,128)}) %all-gather.4.cloned.1.call-update) | async-done | bytes 1048592 | tf_op jit(solution)/shard_map/all_gather | solution.py:211
  75.1 122.3 %shard_map.37 = (f32[3,512,640]{2,1,0:T(8,128)}, f32[512,640]{1,0:T(8,128)}, f32[512,512]{1,0:T(8,128)}) custom-call(s32[2]{0:T(128)} %pad_add_fusion.side_ref, f32[4,4,136,512]{3,2,1,0:T(8,128)} %bitcast.6, f32[4,512,128]{2,1,0:T(8,128)} %all-gather.4.cloned.1.call-done.rhs), custom_call_target="tpu_custom_call" | custom-call | tf_op jit(solution)/shard_map/pallas_call | solution.py:221
  197.4 0.0 collective-permute-done.from_right
  197.4 0.0 copy-start.1
  197.4 1.1 copy-done.1
  198.5 37.6 %shard_map.38 = (f32[512,640]{1,0:T(8,128)}, f32[512,640]{1,0:T(8,128)}) custom-call(s32[2]{0:T(128)} %pad_add_fusion.side_ref, f32[4,4,136,512]{3,2,1,0:T(8,128)} %bitcast.7, f32[1,4,136,512]{3,2,1,0:T(8,128)} %copy-done.1, f32[4,512,128]{2,1,0:T(8,128)} %all-gather.4.cloned.1.call-done.rhs, f32[512,640]{1,0:T(8,128)} %get-tuple-element.10.carry, ...), custom_call_target="tpu_custom_call" | custom-call | tf_op jit(solution)/shard_map/pallas_call | solution.py:230
  236.0 3.0 collective-permute-start.1
  239.1 57.1 %collective-permute-done.1.received = f32[512,640]{1,0:T(8,128)S(1)} collective-permute-done((f32[512,640]{1,0:T(8,128)}, f32[512,640]{1,0:T(8,128)S(1)}, u32[]{:S(2)}, u32[]{:S(2)}) %collective-permute-start.1) | collective-permute-done | bytes 1310752 | tf_op jit(solution)/shard_map/ppermute | solution.py:240
  296.2 0.0 copy-start
  296.2 1.1 copy-done
  297.3 27.1 %shard_map.39 = f32[512,128]{1,0:T(8,128)} custom-call(s32[2]{0:T(128)} %pad_add_fusion.side_ref, f32[512,640]{1,0:T(8,128)} %get-tuple-element.12.reduced, f32[512,640]{1,0:T(8,128)} %copy-done, f32[3,512,640]{2,1,0:T(8,128)} %get-tuple-element.14.solved), custom_call_target="tpu_custom_call" | custom-call | tf_op jit(solution)/shard_map/pallas_call | solution.py:242
Async XLA Ops:
  6.5 40.3 %all-gather.6.cloned.1.call-start = ((), (), s32[]{:S(2)}) async-start(), calls=%async_computation.1 | async-start | bytes 4734976 | tf_op jit(solution)/shard_map/all_gather | solution.py:209
  8.3 66.8 %all-gather.4.cloned.1.call-start = ((), (), s32[]{:S(2)}) async-start(), calls=%async_computation | async-start | bytes 1310720 | tf_op jit(solution)/shard_map/all_gather | solution.py:211
  48.2 149.2 %collective-permute-start = (f32[1,4,136,512]{3,2,1,0:T(8,128)S(1)}, f32[1,4,136,512]{3,2,1,0:T(8,128)S(1)}, u32[]{:S(2)}, u32[]{:S(2)}) collective-permute-start(f32[1,4,136,512]{3,2,1,0:T(8,128)S(1)} %bitcast.8), channel_id=1, source_target_pairs={{16,0},{20,4},{24,8},{28,12},{17,1},{21,5},{25,9},{29,13},{18,2},{... | collective-permute-start | bytes 3342344 | tf_op jit(solution)/shard_map/ppermute | solution.py:213
  197.4 1.1 copy-start.1
  236.0 60.2 %collective-permute-start.1 = (f32[512,640]{1,0:T(8,128)}, f32[512,640]{1,0:T(8,128)S(1)}, u32[]{:S(2)}, u32[]{:S(2)}) collective-permute-start(f32[512,640]{1,0:T(8,128)} %get-tuple-element.13), channel_id=1, source_target_pairs={{0,16},{4,20},{8,24},{12,28},{16,0},{20,4},{24,8},{28,12},{1,17},{... | collective-permute-start | bytes 3932168 | tf_op jit(solution)/shard_map/ppermute | solution.py:240
  296.2 1.1 copy-start
Sparse Core Ops, SparseCore 0:
  8.9 37.8 all-gather.5
  48.4 26.6 all-gather.3
